TPU v7x, 256 devices: a whole 4x4x8 slice. The times are simulated.
256 devices in a mesh: aux: 4 (over x), row: 16 (over z_hi, y), col: 4 (over z_lo, core).
Axes of the slice: x: 4, y: 4, z: 8 (z_hi: 4, z_lo: 2; z = z_hi * 2 + z_lo), core: 2. Of those that a mesh axis runs over, the one named last changes fastest.
Arguments:
- factors: bfloat16 [8, 4, 2560, 10240], P('aux', None, 'row', 'col'), may hold values from -0.078125 to 0.078125
- orbitals: bfloat16 [10240, 512], P('col'), may hold values from -0.25 to 0.25
- tile_mask: int32 [8, 80, 80], P('aux'), may hold values from 0 to 1, as said below
Outputs:
- exchange: float32 [10240, 10240], P(('aux', 'row'), 'col')
Inputs may be any that keep to these rules, and one draw needn't show every extreme that they name: `tile_mask`: 0 or 1; present tiles cluster around a centre tile drawn for each auxiliary function, and absent tiles occur everywhere.
All inputs are finite; a program needn't handle non-finite values.
Results may differ from a plain program's by a relative error of at most 0.02.
Values may be sent and summed in bfloat16 or wider, within the bound.
A program may use at most 64 MiB of HBM per device.

v0:
```python
import jax
import jax.numpy as jnp
from jax import lax
from jax.sharding import PartitionSpec as P

NB = 10240
TILE = 128


def on_device(factors, orbitals, tile_mask):
    local_count = factors.shape[0]
    aux_parts = factors.shape[1]
    row_len = factors.shape[2]
    col_len = factors.shape[3]
    occ_count = orbitals.shape[1]
    row_index = lax.axis_index("row")
    col_index = lax.axis_index("col")
    tile_cols = col_len // TILE
    basis_rows = (
        jnp.arange(aux_parts, dtype=jnp.int32)[:, None] * (NB // aux_parts)
        + row_index * row_len
        + jnp.arange(row_len, dtype=jnp.int32)[None, :]
    ) // TILE
    row_tiles = jnp.take(tile_mask, basis_rows, axis=1)
    local_tiles = lax.dynamic_slice_in_dim(row_tiles, col_index * tile_cols, tile_cols, axis=3)
    masked = (
        factors.reshape(local_count, aux_parts, row_len, tile_cols, TILE)
        * local_tiles.astype(jnp.bfloat16)[..., None]
    )
    masked = masked.reshape(factors.shape)
    partial_orb = jnp.einsum("qatn,nk->atqk", masked, orbitals, preferred_element_type=jnp.float32)
    own_panel = lax.psum_scatter(
        partial_orb.astype(jnp.bfloat16), "col", scatter_dimension=0, tiled=True
    )
    row_panel = lax.all_gather(own_panel, "col", axis=0, tiled=True)
    rows_three = row_panel.reshape(aux_parts * row_len, local_count, occ_count)
    cols_three = own_panel.reshape(row_len, local_count, occ_count)
    zeros_k = jnp.zeros((aux_parts * row_len, col_len), jnp.float32)

    def one_function(function_index, summed):
        left_rows = lax.dynamic_index_in_dim(rows_three, function_index, 1, keepdims=False)
        right_rows = lax.dynamic_index_in_dim(cols_three, function_index, 1, keepdims=False)
        return summed + lax.dot_general(
            left_rows,
            lax.all_gather(right_rows, "row", axis=0, tiled=True),
            (((1,), (1,)), ((), ())),
            preferred_element_type=jnp.float32,
        )

    partial_k = lax.fori_loop(0, local_count, one_function, zeros_k)
    return lax.psum_scatter(
        partial_k.astype(jnp.bfloat16), "aux", scatter_dimension=0, tiled=True
    ).astype(jnp.float32)


def solution(mesh):
    placed = (P("aux", None, "row", "col"), P("col", None), P("aux", None, None))
    return jax.shard_map(
        on_device, mesh=mesh, in_specs=placed, out_specs=P(("aux", "row"), "col"), check_vma=False
    )
```

profile of v0, /device:TPU:1, one launch (start us, length us, event | category | flops | bytes accessed | tf_op | source)
XLA Modules:
  0.0 320.6 jit_solution(14469421907034454084)
XLA Ops:
  6.5 0.0 copy-start
  6.5 0.0 all-reduce.3.cloned.1.call-start
  6.5 0.1 compare_select_fusion
  6.6 0.1 compare_and_fusion
  6.7 0.1 reshape.123
  6.8 3.4 %gather_fusion = s32[640,2,80]{2,0,1:T(8,128)S(1)} fusion(s32[2,80,80]{2,1,0:T(8,128)} %param.7, s32[1024]{0:T(1024)S(1)} %pad_clamp_fusion), kind=kCustom, calls=%fused_computation | custom fusion | bytes 821760 | tf_op jit(solution)/shard_map/jit(_take)/gather | solution.py:24
  10.2 0.3 fusion.18
  10.5 6.8 %mul.28 = bf16[2,4,160,20,128]{4,3,2,1,0:T(8,128)(2,1)} broadcast(bf16[2,4,160,20]{3,2,1,0:T(8,128)(2,1)S(1)} %fusion.18), dimensions={0,1,2,3} | broadcast | bytes 6604800 | tf_op jit(solution)/shard_map/mul | solution.py:27
  17.3 12.0 %mul.29 = bf16[2,4,160,2560]{3,2,1,0:T(8,128)(2,1)} reshape(bf16[2,4,160,20,128]{4,3,2,1,0:T(8,128)(2,1)} %mul.28) | data formatting | bytes 13107200 | tf_op jit(solution)/shard_map/mul | solution.py:27
  29.3 9.4 %fusion.12 = bf16[4,160,2,512]{3,1,0,2:T(8,128)(2,1)} fusion(bf16[2560,512]{1,0:T(8,128)(2,1)S(1)} %copy-done, bf16[2,4,160,2560]{3,2,1,0:T(8,128)(2,1)} %param.5, bf16[2,4,160,2560]{3,2,1,0:T(8,128)(2,1)} %mul.29), kind=kOutput, calls=%fused_computation.11 | convolution fusion | flops 3359375360 | bytes 17039360 | tf_op jit(solution)/shard_map/qatn,nk->atqk/dot_general | solution.py:31
  38.6 0.0 all-reduce.3.cloned.1.call-update
  38.7 0.0 all-gather.7.cloned.1.call-start
  38.7 0.6 dynamic-slice.1
  39.3 53.3 %all-reduce.3.cloned.1.call-done = bf16[4,160,2,512]{3,1,0,2:T(8,128)(2,1)} async-done(((bf16[4,160,2,512]{3,1,0,2:T(8,128)(2,1)}), bf16[4,160,2,512]{3,1,0,2:T(8,128)(2,1)}) %all-reduce.3.cloned.1.call-update) | async-done | bytes 1310736
  92.6 2.4 constant_dynamic-slice_fusion.1
  95.0 0.0 all-gather.7.cloned.1.call-update
  95.0 1.6 fusion.25
  96.6 24.2 %all-gather.7.cloned.1.call-done = bf16[4,160,2,512]{3,1,0,2:T(8,128)(2,1)} async-done(((bf16[1,160,2,512]{3,1,0,2:T(8,128)(2,1)}), bf16[4,160,2,512]{3,1,0,2:T(8,128)(2,1)}) %all-gather.7.cloned.1.call-update) | async-done | bytes 1310736 | tf_op jit(solution)/shard_map/all_gather | solution.py:35
  120.9 145.5 %while.14 = (s32[]{:T(128)}, f32[640,2560]{1,0:T(8,128)}, bf16[640,2,512]{2,0,1:T(8,128)(2,1)}, bf16[160,2,512]{2,0,1:T(8,128)(2,1)S(1)}, s32[]{:T(128)}, /*index=5*/s32[]{:T(128)}) while((s32[]{:T(128)}, f32[640,2560]{1,0:T(8,128)}, bf16[640,2,512]{2,0,1:T(8,128)(2,1)}, bf16[160,2,512]{2,0,1:T(8,128)(2,1)S(1)}, s32[]{:T(128)}, ...), condition=%wide.region_2.3_spmd.clone, body=%wide.region_1.2_spmd.clone.sunk | while | flops 1680998400 | bytes 25067656 | solution.py:50
  120.9 0.0 all-gather.9.cloned.1.call-start
  120.9 0.7 constant_dynamic-slice_fusion.3
  121.6 0.0 all-gather.9.cloned.1.call-update
  121.6 65.5 %all-gather.9.cloned.1.call-done = bf16[2560,1,512]{2,0,1:T(8,128)(2,1)} async-done(((bf16[160,1,512]{2,0,1:T(8,128)(2,1)}), bf16[2560,1,512]{2,0,1:T(8,128)(2,1)}) %all-gather.9.cloned.1.call-update) | async-done | bytes 2621456 | tf_op jit(solution)/shard_map/while/body/eval_jaxpr/all_gather | solution.py:45
  187.1 6.6 %select_add_fusion.2 = f32[640,2560]{1,0:T(8,128)} fusion(f32[640,2560]{1,0:T(8,128)} %get-tuple-element.144, pred[]{:T(512)S(6)} %compare.17, bf16[2560,1,512]{2,0,1:T(8,128)(2,1)} %all-gather.9.cloned.1.call-done, bf16[640,2,512]{2,0,1:T(8,128)(2,1)} %get-tuple-element.151, s32[]{:T(128)S(6)} %copy.12), kind=kOutput, calls=%fused_computation.1.clone.1 | convolution fusion | flops 1680998400 | bytes 16384005 | tf_op jit(solution)/shard_map/while/body/eval_jaxpr/dot_general | solution.py:43
  193.7 0.7 constant_dynamic-slice_fusion.3
  194.4 0.0 all-gather.9.cloned.1.call-update
  194.4 63.4 %all-gather.9.cloned.1.call-done = bf16[2560,1,512]{2,0,1:T(8,128)(2,1)} async-done(((bf16[160,1,512]{2,0,1:T(8,128)(2,1)}), bf16[2560,1,512]{2,0,1:T(8,128)(2,1)}) %all-gather.9.cloned.1.call-update) | async-done | bytes 2621456 | tf_op jit(solution)/shard_map/while/body/eval_jaxpr/all_gather | solution.py:45
  257.9 8.5 %select_add_fusion.2 = f32[640,2560]{1,0:T(8,128)} fusion(f32[640,2560]{1,0:T(8,128)} %get-tuple-element.144, pred[]{:T(512)S(6)} %compare.17, bf16[2560,1,512]{2,0,1:T(8,128)(2,1)} %all-gather.9.cloned.1.call-done, bf16[640,2,512]{2,0,1:T(8,128)(2,1)} %get-tuple-element.151, s32[]{:T(128)S(6)} %copy.12), kind=kOutput, calls=%fused_computation.1.clone.1 | convolution fusion | flops 1680998400 | bytes 16384005 | tf_op jit(solution)/shard_map/while/body/eval_jaxpr/dot_general | solution.py:43
  266.4 5.0 %convert_element_type.18 = bf16[640,2560]{1,0:T(8,128)(2,1)} convert(f32[640,2560]{1,0:T(8,128)} %get-tuple-element.84) | non-fusion elementwise | flops 1638400 | bytes 9830400 | tf_op jit(solution)/shard_map/convert_element_type | solution.py:52
  271.4 0.0 reduce-scatter.5.cloned.1.call-update
  271.4 40.2 %reduce-scatter.5.cloned.1.call-done = bf16[160,2560]{1,0:T(8,128)(2,1)} async-done(((bf16[640,2560]{1,0:T(8,128)(2,1)}), bf16[160,2560]{1,0:T(8,128)(2,1)}) %reduce-scatter.5.cloned.1.call-update) | async-done | bytes 819216 | tf_op jit(solution)/shard_map/reduce_scatter | solution.py:51
  311.6 2.5 convert_element_type.19
  (8 shorter events, 0.0 us)
Async XLA Ops:
  6.5 22.7 %copy-start = (bf16[2560,512]{1,0:T(8,128)(2,1)S(1)}, bf16[2560,512]{1,0:T(8,128)(2,1)}, u32[]{:S(2)}) copy-start(bf16[2560,512]{1,0:T(8,128)(2,1)} %param.6) | copy-start | bytes 7864324
  6.5 86.1 %all-reduce.3.cloned.1.call-start = ((), (), s32[]{:S(2)}) async-start(), calls=%async_computation.3 | async-start | bytes 2621440
  29.3 9.4 %copy-start.1 = (u32[256]{0:T(256)S(1)}, u32[256]{0:T(256)}, u32[]{:S(2)}) copy-start(u32[256]{0:T(256)} %constant.82) | copy-start | bytes 3076
  38.7 82.2 %all-gather.7.cloned.1.call-start = ((), (), s32[]{:S(2)}) async-start(), calls=%async_computation.1 | async-start | bytes 1638400 | tf_op jit(solution)/shard_map/all_gather | solution.py:35
  120.9 66.3 %all-gather.9.cloned.1.call-start = ((), (), s32[]{:S(2)}) async-start(), calls=%async_computation.4 | async-start | bytes 2785280 | tf_op jit(solution)/shard_map/while/body/eval_jaxpr/all_gather | solution.py:45
  193.7 64.2 %all-gather.9.cloned.1.call-start = ((), (), s32[]{:S(2)}) async-start(), calls=%async_computation.4 | async-start | bytes 2785280 | tf_op jit(solution)/shard_map/while/body/eval_jaxpr/all_gather | solution.py:45
  266.4 45.2 %reduce-scatter.5.cloned.1.call-start = ((), (), s32[]{:S(2)}) async-start(), calls=%async_computation.2 | async-start | bytes 4096000 | tf_op jit(solution)/shard_map/reduce_scatter | solution.py:51
Sparse Core Ops, SparseCore 0:
  38.8 53.7 all-reduce.2
  95.1 25.7 all-gather.6
  124.1 62.9 all-gather.8
  196.7 61.1 all-gather.8
  271.5 40.0 reduce-scatter.4
where the time goes:
time: 321 us
  waiting for transfers between devices  247 us (77%)
  local copies, waits for them, and re-layouts  28.2 us (9%)
  matrix products  24.4 us (8%)
  between operations  13.2 us (4%)
  other arithmetic  7.97 us (2%)
    all_gather x2, waiting for transfers between devices, one_function(): lax.all_gather(right_rows, 'row', axis=0, tiled=True)  129 us
    unnamed x4, waiting for transfers between devices  53.3 us
    reduce_scatter x1, waiting for transfers between devices, on_device(): lax.psum_scatter(partial_k.astype(jnp.bfloat16), 'aux', scatter_dimension...  40.2 us
    all_gather x1, waiting for transfers between devices, on_device(): row_panel = lax.all_gather(own_panel, 'col', axis=0, tiled=True)  24.2 us
    mul x2, local copies, waits for them, and re-layouts, on_device(): factors.reshape(local_count, aux_parts, row_len, tile_cols, TILE)  18.7 us
    dot_general x2, matrix products, one_function(): lax.dot_general(left_rows, lax.all_gather(right_rows, 'row', axis=0, tile...  15.1 us
    dot_general x1, matrix products, on_device(): jnp.einsum('qatn,nk->atqk', masked, orbitals, preferred_element_type=jnp....  9.36 us
  transfers between devices with their start and end apart: 5, of which 5 were waited for; matrix products, arithmetic and copies ran while one was open for 1% of the time, Pallas kernels for 0%

commit v1 on v0

--- a/solution.py
+++ b/solution.py
@@ -40,9 +40,12 @@
     def one_function(function_index, summed):
         left_rows = lax.dynamic_index_in_dim(rows_three, function_index, 1, keepdims=False)
         right_rows = lax.dynamic_index_in_dim(cols_three, function_index, 1, keepdims=False)
+        _end_screen = lambda vec, d0: jnp.concatenate(
+            jax.lax.all_to_all(jnp.stack(jax.lax.axis_size("row") * [vec], 0), "row", 0, 0), d0
+        )
         return summed + lax.dot_general(
             left_rows,
-            lax.all_gather(right_rows, "row", axis=0, tiled=True),
+            _end_screen(right_rows, d0=0),
             (((1,), (1,)), ((), ())),
             preferred_element_type=jnp.float32,
         )

time: 321 us -> 332 us (1.034)
  starting transfers between devices: 0.05 us -> 21.5 us
  waiting for transfers between devices: 247 us -> 234 us
    all_gather x2 -> x0, waiting for transfers between devices: 129 us -> none  [one_function(): lax.all_gather(right_rows, 'row', axis=0, tiled=True)]
    all_to_all x0 -> x2, waiting for transfers between devices: none -> 97.6 us  [one_function(): jax.lax.all_to_all(jnp.stack(jax.lax.axis_size('row') * [vec], 0), 'row',...]
    all_to_all x0 -> x2, starting transfers between devices: none -> 21.4 us  [one_function(): jax.lax.all_to_all(jnp.stack(jax.lax.axis_size('row') * [vec], 0), 'row',...]
    reduce_scatter x1, waiting for transfers between devices: 40.2 us -> 59.2 us  [on_device(): lax.psum_scatter(partial_k.astype(jnp.bfloat16), 'aux', scatter_dimension...]
    another operation x0 -> x4, local copies, waits for them, and re-layouts: none -> 3.46 us  [one_function(): jnp.stack(jax.lax.axis_size('row') * [vec], 0)]
where the time goes in v1:
time: 332 us
  waiting for transfers between devices  234 us (70%)
  local copies, waits for them, and re-layouts  30.4 us (9%)
  matrix products  24.5 us (7%)
  starting transfers between devices  21.5 us (6%)
  between operations  13.2 us (4%)
  other arithmetic  7.95 us (2%)
    all_to_all x2, waiting for transfers between devices, one_function(): jax.lax.all_to_all(jnp.stack(jax.lax.axis_size('row') * [vec], 0), 'row',...  97.6 us
    reduce_scatter x1, waiting for transfers between devices, on_device(): lax.psum_scatter(partial_k.astype(jnp.bfloat16), 'aux', scatter_dimension...  59.2 us
    unnamed x4, waiting for transfers between devices  53.2 us
    all_gather x1, waiting for transfers between devices, on_device(): row_panel = lax.all_gather(own_panel, 'col', axis=0, tiled=True)  24.1 us
    all_to_all x2, starting transfers between devices, one_function(): jax.lax.all_to_all(jnp.stack(jax.lax.axis_size('row') * [vec], 0), 'row',...  21.4 us
    mul x2, local copies, waits for them, and re-layouts, on_device(): factors.reshape(local_count, aux_parts, row_len, tile_cols, TILE)  18.7 us
    dot_general x2, matrix products, one_function(): lax.dot_general(left_rows, _end_screen(right_rows, d0=0), (((1,), (1,)),...  15.1 us
    dot_general x1, matrix products, on_device(): jnp.einsum('qatn,nk->atqk', masked, orbitals, preferred_element_type=jnp....  9.36 us
  transfers between devices with their start and end apart: 5, of which 5 were waited for; matrix products, arithmetic and copies ran while one was open for 1% of the time, Pallas kernels for 0%

profile of v1, /device:TPU:1, one launch (start us, length us, event | category | flops | bytes accessed | tf_op | source)
XLA Modules:
  0.0 331.8 jit_solution(14648665257185578240)
XLA Ops:
  6.5 0.0 copy-start
  6.5 0.1 compare_select_fusion
  6.6 0.1 compare_and_fusion
  6.7 0.1 reshape.135
  6.8 3.4 %gather_fusion = s32[640,2,80]{2,0,1:T(8,128)S(1)} fusion(s32[2,80,80]{2,1,0:T(8,128)} %param.7, s32[1024]{0:T(1024)S(1)} %pad_clamp_fusion), kind=kCustom, calls=%fused_computation | custom fusion | bytes 821760 | tf_op jit(solution)/shard_map/jit(_take)/gather | solution.py:24
  10.2 0.3 fusion.17
  10.5 6.8 %mul.28 = bf16[2,4,160,20,128]{4,3,2,1,0:T(8,128)(2,1)} broadcast(bf16[2,4,160,20]{3,2,1,0:T(8,128)(2,1)S(1)} %fusion.17), dimensions={0,1,2,3} | broadcast | bytes 6604800 | tf_op jit(solution)/shard_map/mul | solution.py:27
  17.3 12.0 %mul.29 = bf16[2,4,160,2560]{3,2,1,0:T(8,128)(2,1)} reshape(bf16[2,4,160,20,128]{4,3,2,1,0:T(8,128)(2,1)} %mul.28) | data formatting | bytes 13107200 | tf_op jit(solution)/shard_map/mul | solution.py:27
  29.3 9.4 %fusion.11 = bf16[4,160,2,512]{3,1,0,2:T(8,128)(2,1)} fusion(bf16[2560,512]{1,0:T(8,128)(2,1)S(1)} %copy-done, bf16[2,4,160,2560]{3,2,1,0:T(8,128)(2,1)} %param.5, bf16[2,4,160,2560]{3,2,1,0:T(8,128)(2,1)} %mul.29), kind=kOutput, calls=%fused_computation.10 | convolution fusion | flops 3359375360 | bytes 17039360 | tf_op jit(solution)/shard_map/qatn,nk->atqk/dot_general | solution.py:31
  38.6 0.0 all-reduce.3.cloned.1.call-update
  38.7 0.0 all-gather.2.cloned.1.call-start
  38.7 0.0 copy-done.1
  38.7 0.7 dynamic-slice.1
  39.4 53.2 %all-reduce.3.cloned.1.call-done = bf16[4,160,2,512]{3,1,0,2:T(8,128)(2,1)} async-done(((bf16[4,160,2,512]{3,1,0,2:T(8,128)(2,1)}), bf16[4,160,2,512]{3,1,0,2:T(8,128)(2,1)}) %all-reduce.3.cloned.1.call-update) | async-done | bytes 1310736
  92.6 2.4 constant_dynamic-slice_fusion
  95.0 0.0 all-gather.2.cloned.1.call-update
  95.0 0.0 reduce-scatter.5.cloned.1.call-start
  95.1 1.7 fusion.25
  96.8 24.1 %all-gather.2.cloned.1.call-done = bf16[4,160,2,512]{3,1,0,2:T(8,128)(2,1)} async-done(((bf16[1,160,2,512]{3,1,0,2:T(8,128)(2,1)}), bf16[4,160,2,512]{3,1,0,2:T(8,128)(2,1)}) %all-gather.2.cloned.1.call-update) | async-done | bytes 1310736 | tf_op jit(solution)/shard_map/all_gather | solution.py:35
  120.9 137.7 %while.14 = (s32[]{:T(128)}, f32[640,2560]{1,0:T(8,128)}, bf16[640,2,512]{2,0,1:T(8,128)(2,1)}, bf16[160,2,512]{2,0,1:T(8,128)(2,1)S(1)}, s32[]{:T(128)}, /*index=5*/s32[]{:T(128)}) while((s32[]{:T(128)}, f32[640,2560]{1,0:T(8,128)}, bf16[640,2,512]{2,0,1:T(8,128)(2,1)}, bf16[160,2,512]{2,0,1:T(8,128)(2,1)S(1)}, s32[]{:T(128)}, ...), condition=%wide.region_2.3_spmd.clone, body=%wide.region_1.2_spmd.clone.sunk | while | flops 1680998400 | bytes 27361408 | solution.py:53
  120.9 1.7 stack.11
  122.7 8.4 %all-to-all-start = ((bf16[16,160,512]{2,1,0:T(8,128)(2,1)}), bf16[16,160,512]{2,1,0:T(8,128)(2,1)}, u32[]{:S(2)}, u32[]{:S(2)}) async-start(bf16[16,160,512]{2,1,0:T(8,128)(2,1)} %stack.11), calls=%async_computation | async-start | bytes 5242880 | tf_op jit(solution)/shard_map/while/body/eval_jaxpr/all_to_all | solution.py:44
  131.1 50.9 %all-to-all-done = bf16[16,160,512]{2,1,0:T(8,128)(2,1)} async-done(((bf16[16,160,512]{2,1,0:T(8,128)(2,1)}), bf16[16,160,512]{2,1,0:T(8,128)(2,1)}, u32[]{:S(2)}, u32[]{:S(2)}) %all-to-all-start) | async-done | bytes 2621472 | tf_op jit(solution)/shard_map/while/body/eval_jaxpr/all_to_all | solution.py:44
  182.0 6.6 %select_add_fusion.2 = f32[640,2560]{1,0:T(8,128)} fusion(f32[640,2560]{1,0:T(8,128)} %get-tuple-element.144, bf16[2560,512]{1,0:T(8,128)(2,1)} %bitcast.42, pred[]{:T(512)S(6)} %compare.17, bf16[640,2,512]{2,0,1:T(8,128)(2,1)} %get-tuple-element.151, s32[]{:T(128)S(6)} %copy.12), kind=kOutput, calls=%fused_computation.1.clone.1 | convolution fusion | flops 1680998400 | bytes 16384005 | tf_op jit(solution)/shard_map/while/body/eval_jaxpr/dot_general | solution.py:46
  188.6 1.7 stack.11
  190.3 13.0 %all-to-all-start = ((bf16[16,160,512]{2,1,0:T(8,128)(2,1)}), bf16[16,160,512]{2,1,0:T(8,128)(2,1)}, u32[]{:S(2)}, u32[]{:S(2)}) async-start(bf16[16,160,512]{2,1,0:T(8,128)(2,1)} %stack.11), calls=%async_computation | async-start | bytes 5242880 | tf_op jit(solution)/shard_map/while/body/eval_jaxpr/all_to_all | solution.py:44
  203.3 46.8 %all-to-all-done = bf16[16,160,512]{2,1,0:T(8,128)(2,1)} async-done(((bf16[16,160,512]{2,1,0:T(8,128)(2,1)}), bf16[16,160,512]{2,1,0:T(8,128)(2,1)}, u32[]{:S(2)}, u32[]{:S(2)}) %all-to-all-start) | async-done | bytes 2621472 | tf_op jit(solution)/shard_map/while/body/eval_jaxpr/all_to_all | solution.py:44
  250.1 8.5 %select_add_fusion.2 = f32[640,2560]{1,0:T(8,128)} fusion(f32[640,2560]{1,0:T(8,128)} %get-tuple-element.144, bf16[2560,512]{1,0:T(8,128)(2,1)} %bitcast.42, pred[]{:T(512)S(6)} %compare.17, bf16[640,2,512]{2,0,1:T(8,128)(2,1)} %get-tuple-element.151, s32[]{:T(128)S(6)} %copy.12), kind=kOutput, calls=%fused_computation.1.clone.1 | convolution fusion | flops 1680998400 | bytes 16384005 | tf_op jit(solution)/shard_map/while/body/eval_jaxpr/dot_general | solution.py:46
  258.6 5.0 %convert_element_type.18 = bf16[640,2560]{1,0:T(8,128)(2,1)} convert(f32[640,2560]{1,0:T(8,128)} %get-tuple-element.84) | non-fusion elementwise | flops 1638400 | bytes 9830400 | tf_op jit(solution)/shard_map/convert_element_type | solution.py:55
  263.6 0.0 reduce-scatter.5.cloned.1.call-update
  263.6 59.2 %reduce-scatter.5.cloned.1.call-done = bf16[160,2560]{1,0:T(8,128)(2,1)} async-done(((bf16[640,2560]{1,0:T(8,128)(2,1)}), bf16[160,2560]{1,0:T(8,128)(2,1)}) %reduce-scatter.5.cloned.1.call-update) | async-done | bytes 819216 | tf_op jit(solution)/shard_map/reduce_scatter | solution.py:54
  322.7 2.5 convert_element_type.19
  (8 shorter events, 0.0 us)
Async XLA Ops:
  6.5 22.7 %copy-start = (bf16[2560,512]{1,0:T(8,128)(2,1)S(1)}, bf16[2560,512]{1,0:T(8,128)(2,1)}, u32[]{:S(2)}) copy-start(bf16[2560,512]{1,0:T(8,128)(2,1)} %param.6) | copy-start | bytes 7864324
  6.5 86.1 %all-reduce.3.cloned.1.call-start = ((), (), s32[]{:S(2)}) async-start(), calls=%async_computation.4 | async-start | bytes 2621440
  29.3 9.4 %copy-start.1 = (u32[256]{0:T(256)S(1)}, u32[256]{0:T(256)}, u32[]{:S(2)}) copy-start(u32[256]{0:T(256)} %constant.82) | copy-start | bytes 3076
  38.7 82.3 %all-gather.2.cloned.1.call-start = ((), (), s32[]{:S(2)}) async-start(), calls=%async_computation.2 | async-start | bytes 1638400 | tf_op jit(solution)/shard_map/all_gather | solution.py:35
  95.0 227.7 %reduce-scatter.5.cloned.1.call-start = ((), (), s32[]{:S(2)}) async-start(), calls=%async_computation.3 | async-start | bytes 4096000 | tf_op jit(solution)/shard_map/reduce_scatter | solution.py:54
  122.7 59.3 %all-to-all-start = ((bf16[16,160,512]{2,1,0:T(8,128)(2,1)}), bf16[16,160,512]{2,1,0:T(8,128)(2,1)}, u32[]{:S(2)}, u32[]{:S(2)}) async-start(bf16[16,160,512]{2,1,0:T(8,128)(2,1)} %stack.11), calls=%async_computation | async-start | bytes 5242880 | tf_op jit(solution)/shard_map/while/body/eval_jaxpr/all_to_all | solution.py:44
  190.3 59.8 %all-to-all-start = ((bf16[16,160,512]{2,1,0:T(8,128)(2,1)}), bf16[16,160,512]{2,1,0:T(8,128)(2,1)}, u32[]{:S(2)}, u32[]{:S(2)}) async-start(bf16[16,160,512]{2,1,0:T(8,128)(2,1)} %stack.11), calls=%async_computation | async-start | bytes 5242880 | tf_op jit(solution)/shard_map/while/body/eval_jaxpr/all_to_all | solution.py:44
Sparse Core Ops, SparseCore 0:
  38.8 53.7 all-reduce.2
  95.1 25.7 all-gather.1
  263.7 59.0 reduce-scatter.4
